TPU v7x, 32 devices: a whole 2x2x4 slice. The times are simulated.
32 devices in a mesh: groups: 2 (over x), ctx: 8 (over z, y), dp: 2 (over core).
Axes of the slice: x: 2, y: 2, z: 4, core: 2. Of those that a mesh axis runs over, the one named last changes fastest.
Arguments:
- tokens: bfloat16 [8, 1024, 4096], P(('groups', 'dp'), 'ctx'), parts along dimension 0, may hold values from -6 to 6
- norm_gain: float32 [4096], replicated, may hold values from 0.25 to 1.75
- w_query: bfloat16 [4096, 2048], P('dp')
- w_key: bfloat16 [4096, 2048], P('dp')
- w_value: bfloat16 [4096, 2048], P('dp'), may hold values from -0.09375 to 0.09375
- query_gain: float32 [2048], replicated
- key_gain: float32 [2048], replicated
- key_blocks: int32 [16, 5], P(('groups', 'ctx')), parts along dimension 0, may hold values from 0 to 7, as said below
Outputs:
- attended: bfloat16 [8, 1024, 2048], P(('groups', 'dp'), 'ctx'), parts along dimension 0
There are 2 independent parts, one for each index of `groups`. A program takes and returns all parts, laid end to end along the dimension named above; an argument that names none is the same for every part. Nothing has to cross between parts.
Inputs may be any that keep to these rules, and one draw needn't show every extreme that they name: `key_blocks`: row b holds b - 1, b, b + 1 (modulo 8) and then two different blocks (b + 2 m) modulo 8 with m from 1 to 3.
All inputs are finite; a program needn't handle non-finite values.
Results may differ from a plain program's by a relative error of at most 0.012.
The roundings to bfloat16 on the way count: a program that leaves them out, or rounds other values in their place, can miss the bound.
Values may be sent and summed in bfloat16 or wider, within the bound.
A program may use at most 256 MiB of HBM per device.

v0:
```python
import jax
import jax.numpy as jnp
from jax import lax
from jax.sharding import PartitionSpec as P

HEAD_DIM = 128


def head_norm(tensor, gain_row, seq_count, block_len):
    head_count = gain_row.shape[0] // HEAD_DIM
    shaped = tensor.reshape(seq_count, block_len, head_count, HEAD_DIM)
    mean_sq = jnp.mean(shaped * shaped, axis=-1, keepdims=True)
    gains = gain_row.reshape(head_count, HEAD_DIM)
    return (shaped * lax.rsqrt(mean_sq + 1e-06) * gains).astype(jnp.bfloat16)


def shards(tokens, norm_gain, w_query, w_key, w_value, query_gain, key_gain, key_blocks):
    seq_count, block_len, feature_width = tokens.shape
    all_heads = w_query.shape[1]
    head_count = all_heads // HEAD_DIM
    wide = tokens.astype(jnp.float32)
    mean_sq = jnp.mean(wide * wide, axis=-1, keepdims=True)
    normed = (wide * lax.rsqrt(mean_sq + 1e-06) * norm_gain).astype(jnp.bfloat16)
    flat_rows = normed.reshape(seq_count * block_len, feature_width)
    pieces = (
        lax.all_gather(w_query, "dp", axis=0, tiled=True),
        lax.all_gather(w_key, "dp", axis=0, tiled=True),
        lax.all_gather(w_value, "dp", axis=0, tiled=True),
    )
    query_raw, key_raw, value_raw = tuple(
        (jnp.dot(flat_rows, piece, preferred_element_type=jnp.float32) for piece in pieces)
    )
    queries = head_norm(query_raw, query_gain, seq_count, block_len)
    keys_here = head_norm(key_raw, key_gain, seq_count, block_len).reshape(
        seq_count, block_len, all_heads
    )
    values_here = value_raw.astype(jnp.bfloat16).reshape(seq_count, block_len, all_heads)
    key_value = jnp.stack([keys_here, values_here], axis=0)
    listed = key_blocks[0]
    slot_count = listed.shape[0]
    cycle_size = lax.axis_size("ctx")
    slot_ids = jnp.arange(slot_count, dtype=jnp.int32)
    slot_store = jnp.zeros((2, seq_count, slot_count, block_len, all_heads), jnp.bfloat16)
    piece = lax.all_gather(key_value, "ctx", axis=2, tiled=True)
    block_count = piece.shape[2] // block_len
    shaped = piece.reshape(2, seq_count, block_count, block_len, all_heads)
    first_block = jnp.floor_divide(jnp.int32(0), block_len)

    def put_one(which, current_store):
        source = jnp.mod(first_block + which, cycle_size)
        matches = listed == source
        slot = jnp.sum(jnp.where(matches, slot_ids, 0))
        present = jnp.any(matches)
        arriving = lax.dynamic_slice_in_dim(shaped, which, 1, 2)
        existing = lax.dynamic_slice_in_dim(current_store, slot, 1, 2)
        return lax.dynamic_update_slice_in_dim(
            current_store, jnp.where(present, arriving, existing), slot, 2
        )

    slot_store = lax.fori_loop(0, block_count, put_one, slot_store)
    key_rows = slot_store[0].reshape(seq_count, slot_count * block_len, head_count, HEAD_DIM)
    value_rows = slot_store[1].reshape(seq_count, slot_count * block_len, head_count, HEAD_DIM)
    score_scale = 1.0 / float(HEAD_DIM) ** 0.5
    scores = (
        jnp.einsum("sqhd,skhd->shqk", queries, key_rows, preferred_element_type=jnp.float32)
        * score_scale
    )
    row_max = jnp.max(scores, axis=-1, keepdims=True)
    expo = jnp.exp(scores - row_max)
    total_weight = jnp.sum(expo, axis=-1, keepdims=True)
    weights = expo.astype(jnp.bfloat16)
    mixed = jnp.einsum("shqk,skhd->sqhd", weights, value_rows, preferred_element_type=jnp.float32)
    mixed = mixed / jnp.transpose(total_weight, (0, 2, 1, 3))
    return mixed.astype(jnp.bfloat16).reshape(seq_count, block_len, all_heads)


def solution(mesh):
    in_specs = (
        P(("groups", "dp"), "ctx", None),
        P(),
        P("dp", None),
        P("dp", None),
        P("dp", None),
        P(),
        P(),
        P(("groups", "ctx"), None),
    )
    out_specs = P(("groups", "dp"), "ctx", None)
    return jax.shard_map(shards, mesh=mesh, in_specs=in_specs, out_specs=out_specs, check_vma=False)
```

profile of v0, /device:TPU:0, one launch (start us, length us, event | category | flops | bytes accessed | tf_op | source)
XLA Modules:
  0.0 474.8 jit_solution(5685028850791455422)
XLA Ops:
  8.8 0.8 copy-done.2
  10.1 2.0 fusion.14
  12.1 29.6 %all-gather.5.cloned.1.call-done = bf16[4096,2048]{1,0:T(8,128)(2,1)} async-done(((bf16[2048,2048]{1,0:T(8,128)(2,1)}), bf16[4096,2048]{1,0:T(8,128)(2,1)}) %all-gather.5.cloned.1.call-update) | async-done | bytes 16777232 | tf_op jit(solution)/shard_map/all_gather | solution.py:27
  41.7 22.1 %copy.16 = bf16[2048,4096]{1,0:T(8,128)(2,1)} copy(bf16[2048,4096]{0,1:T(8,128)(2,1)} %bitcast.55) | data formatting | bytes 33554432 | tf_op jit(solution)/shard_map/dot_general | solution.py:31
  63.8 10.7 %all-gather.7.cloned.1.call-done = bf16[4096,2048]{1,0:T(8,128)(2,1)} async-done(((bf16[2048,2048]{1,0:T(8,128)(2,1)}), bf16[4096,2048]{1,0:T(8,128)(2,1)}) %all-gather.7.cloned.1.call-update) | async-done | bytes 16777232 | tf_op jit(solution)/shard_map/all_gather | solution.py:28
  74.5 9.2 %convolution_convert_fusion = bf16[256,2048]{1,0:T(8,128)(2,1)} fusion(bf16[256,4096]{1,0:T(8,128)(2,1)S(1)} %bitcast.60, bf16[4096,2048]{1,0:T(8,128)(2,1)} %all-gather.7.cloned.1.call-done), kind=kOutput, calls=%fused_computation.20 | convolution fusion | flops 4295491584 | bytes 19922944 | tf_op jit(solution)/shard_map/dot_general | solution.py:31
  83.7 1.7 copy.17
  85.5 12.0 %multiply_reduce_fusion.2 = (f32[2,128,16]{1,2,0:T(8,128)S(1)}, f32[2,128,16,128]{1,3,2,0:T(8,128)S(1)}) fusion(bf16[16,128,4096,1]{2,1,0,3:T(8,128)(2,1)} %bitcast.56, bf16[2,128,4096]{2,1,0:T(8,128)(2,1)S(1)} %copy-done.3), kind=kOutput, calls=%fused_computation.31 | convolution fusion | flops 4296011776 | bytes 20987904 | tf_op jit(solution)/shard_map/dot_general | solution.py:31
  98.0 1.6 pad_maximum_fusion
  99.5 7.8 %all-gather.11.cloned.1.call-done = bf16[4096,2048]{1,0:T(8,128)(2,1)} async-done(((bf16[2048,2048]{1,0:T(8,128)(2,1)}), bf16[4096,2048]{1,0:T(8,128)(2,1)}) %all-gather.11.cloned.1.call-update) | async-done | bytes 16777232 | tf_op jit(solution)/shard_map/all_gather | solution.py:26
  107.4 21.1 %copy.19 = bf16[2048,4096]{1,0:T(8,128)(2,1)} copy(bf16[2048,4096]{0,1:T(8,128)(2,1)} %bitcast.54) | data formatting | bytes 33554432 | tf_op jit(solution)/shard_map/dot_general | solution.py:31
  128.4 9.1 %multiply_reduce_fusion.1 = (f32[2,128,16]{1,2,0:T(8,128)S(1)}, f32[2,128,16,128]{1,3,2,0:T(8,128)}) fusion(bf16[16,128,4096,1]{2,1,0,3:T(8,128)(2,1)} %bitcast.57, bf16[2,128,4096]{2,1,0:T(8,128)(2,1)S(1)} %copy-done.3), kind=kOutput, calls=%fused_computation.29 | convolution fusion | flops 4296011776 | bytes 20987904 | tf_op jit(solution)/shard_map/dot_general | solution.py:31
  137.6 200.6 %all-gather.9.cloned.1.call-done = bf16[2,2,1024,2048]{2,3,1,0:T(8,128)(2,1)} async-done(((bf16[2,2,128,2048]{2,3,1,0:T(8,128)(2,1)}), bf16[2,2,1024,2048]{2,3,1,0:T(8,128)(2,1)}) %all-gather.9.cloned.1.call-update) | async-done | bytes 16777232 | tf_op jit(solution)/shard_map/all_gather | solution.py:44
  338.2 21.9 %copy.18 = bf16[2,2,1024,2048]{3,2,1,0:T(8,128)(2,1)} copy(bf16[2,2,1024,2048]{2,3,1,0:T(8,128)(2,1)} %all-gather.9.cloned.1.call-done) | data formatting | bytes 33554432 | tf_op jit(solution)/shard_map/all_gather | solution.py:44
  360.1 5.3 %broadcast_in_dim.22 = bf16[2,2,5,128,2048]{4,3,2,1,0:T(8,128)(2,1)} broadcast(bf16[]{:T(256)} %constant.91.clone.1), dimensions={} | broadcast | bytes 10485762 | tf_op jit(solution)/shard_map/broadcast_in_dim | solution.py:43
  365.4 67.1 %while.16 = (s32[]{:T(128)}, bf16[2,2,5,128,2048]{4,3,2,1,0:T(8,128)(2,1)}, s32[5]{0:T(128)S(1)}, bf16[2,2,8,128,2048]{4,3,2,1,0:T(8,128)(2,1)}, s32[]{:T(128)},...) while((s32[]{:T(128)}, bf16[2,2,5,128,2048]{4,3,2,1,0:T(8,128)(2,1)}, s32[5]{0:T(128)S(1)}, ...), condition=%wide.region_5.6_spmd.clone, body=%wide.region_2.5_spmd.clone.sunk | while | flops 1048610 | bytes 6292722 | solution.py:60
  368.6 5.1 %select_dynamic-update-slice_fusion.2 = bf16[2,2,5,128,2048]{4,3,2,1,0:T(8,128)(2,1)} fusion(bf16[2,2,5,128,2048]{4,3,2,1,0:T(8,128)(2,1)} %get-tuple-element.218, s32[]{:T(128)S(6)} %select_n.93, bf16[2,2,8,128,2048]{4,3,2,1,0:T(8,128)(2,1)} %get-tuple-element.229, s32[]{:T(128)} %get-tuple-element.217, pred[]{:T(512)} %compare_reduce_fusion.2), kind=kLoop, calls=%fused_computation.1.clone.1 | loop fusion | flops 1048576 | bytes 6292484 | tf_op jit(solution)/shard_map/while/body/eval_jaxpr/dynamic_update_slice | solution.py:56
  377.0 5.1 %select_dynamic-update-slice_fusion.2 = bf16[2,2,5,128,2048]{4,3,2,1,0:T(8,128)(2,1)} fusion(bf16[2,2,5,128,2048]{4,3,2,1,0:T(8,128)(2,1)} %get-tuple-element.218, s32[]{:T(128)S(6)} %select_n.93, bf16[2,2,8,128,2048]{4,3,2,1,0:T(8,128)(2,1)} %get-tuple-element.229, s32[]{:T(128)} %get-tuple-element.217, pred[]{:T(512)} %compare_reduce_fusion.2), kind=kLoop, calls=%fused_computation.1.clone.1 | loop fusion | flops 1048576 | bytes 6292484 | tf_op jit(solution)/shard_map/while/body/eval_jaxpr/dynamic_update_slice | solution.py:56
  385.3 5.1 %select_dynamic-update-slice_fusion.2 = bf16[2,2,5,128,2048]{4,3,2,1,0:T(8,128)(2,1)} fusion(bf16[2,2,5,128,2048]{4,3,2,1,0:T(8,128)(2,1)} %get-tuple-element.218, s32[]{:T(128)S(6)} %select_n.93, bf16[2,2,8,128,2048]{4,3,2,1,0:T(8,128)(2,1)} %get-tuple-element.229, s32[]{:T(128)} %get-tuple-element.217, pred[]{:T(512)} %compare_reduce_fusion.2), kind=kLoop, calls=%fused_computation.1.clone.1 | loop fusion | flops 1048576 | bytes 6292484 | tf_op jit(solution)/shard_map/while/body/eval_jaxpr/dynamic_update_slice | solution.py:56
  393.6 5.2 %select_dynamic-update-slice_fusion.2 = bf16[2,2,5,128,2048]{4,3,2,1,0:T(8,128)(2,1)} fusion(bf16[2,2,5,128,2048]{4,3,2,1,0:T(8,128)(2,1)} %get-tuple-element.218, s32[]{:T(128)S(6)} %select_n.93, bf16[2,2,8,128,2048]{4,3,2,1,0:T(8,128)(2,1)} %get-tuple-element.229, s32[]{:T(128)} %get-tuple-element.217, pred[]{:T(512)} %compare_reduce_fusion.2), kind=kLoop, calls=%fused_computation.1.clone.1 | loop fusion | flops 1048576 | bytes 6292484 | tf_op jit(solution)/shard_map/while/body/eval_jaxpr/dynamic_update_slice | solution.py:56
  402.1 5.2 %select_dynamic-update-slice_fusion.2 = bf16[2,2,5,128,2048]{4,3,2,1,0:T(8,128)(2,1)} fusion(bf16[2,2,5,128,2048]{4,3,2,1,0:T(8,128)(2,1)} %get-tuple-element.218, s32[]{:T(128)S(6)} %select_n.93, bf16[2,2,8,128,2048]{4,3,2,1,0:T(8,128)(2,1)} %get-tuple-element.229, s32[]{:T(128)} %get-tuple-element.217, pred[]{:T(512)} %compare_reduce_fusion.2), kind=kLoop, calls=%fused_computation.1.clone.1 | loop fusion | flops 1048576 | bytes 6292484 | tf_op jit(solution)/shard_map/while/body/eval_jaxpr/dynamic_update_slice | solution.py:56
  410.5 5.2 %select_dynamic-update-slice_fusion.2 = bf16[2,2,5,128,2048]{4,3,2,1,0:T(8,128)(2,1)} fusion(bf16[2,2,5,128,2048]{4,3,2,1,0:T(8,128)(2,1)} %get-tuple-element.218, s32[]{:T(128)S(6)} %select_n.93, bf16[2,2,8,128,2048]{4,3,2,1,0:T(8,128)(2,1)} %get-tuple-element.229, s32[]{:T(128)} %get-tuple-element.217, pred[]{:T(512)} %compare_reduce_fusion.2), kind=kLoop, calls=%fused_computation.1.clone.1 | loop fusion | flops 1048576 | bytes 6292484 | tf_op jit(solution)/shard_map/while/body/eval_jaxpr/dynamic_update_slice | solution.py:56
  418.9 5.1 %select_dynamic-update-slice_fusion.2 = bf16[2,2,5,128,2048]{4,3,2,1,0:T(8,128)(2,1)} fusion(bf16[2,2,5,128,2048]{4,3,2,1,0:T(8,128)(2,1)} %get-tuple-element.218, s32[]{:T(128)S(6)} %select_n.93, bf16[2,2,8,128,2048]{4,3,2,1,0:T(8,128)(2,1)} %get-tuple-element.229, s32[]{:T(128)} %get-tuple-element.217, pred[]{:T(512)} %compare_reduce_fusion.2), kind=kLoop, calls=%fused_computation.1.clone.1 | loop fusion | flops 1048576 | bytes 6292484 | tf_op jit(solution)/shard_map/while/body/eval_jaxpr/dynamic_update_slice | solution.py:56
  427.3 5.2 %select_dynamic-update-slice_fusion.2 = bf16[2,2,5,128,2048]{4,3,2,1,0:T(8,128)(2,1)} fusion(bf16[2,2,5,128,2048]{4,3,2,1,0:T(8,128)(2,1)} %get-tuple-element.218, s32[]{:T(128)S(6)} %select_n.93, bf16[2,2,8,128,2048]{4,3,2,1,0:T(8,128)(2,1)} %get-tuple-element.229, s32[]{:T(128)} %get-tuple-element.217, pred[]{:T(512)} %compare_reduce_fusion.2), kind=kLoop, calls=%fused_computation.1.clone.1 | loop fusion | flops 1048576 | bytes 6292484 | tf_op jit(solution)/shard_map/while/body/eval_jaxpr/dynamic_update_slice | solution.py:56
  432.5 10.2 %fusion.27 = (bf16[1,2,5,128,2048]{4,3,2,1,0:T(8,128)(2,1)}, bf16[1,2,5,128,2048]{4,3,2,1,0:T(8,128)(2,1)}) fusion(bf16[2,2,5,128,2048]{4,3,2,1,0:T(8,128)(2,1)} %get-tuple-element.156), kind=kLoop, calls=%fused_computation.38 | loop fusion | bytes 20971520 | tf_op jit(solution)/shard_map/slice | solution.py:62
  442.7 4.4 copy.27
  447.2 1.8 copy.26
  449.0 5.4 %multiply_reduce_fusion = (f32[2,16,128]{2,1,0:T(8,128)S(1)}, f32[2,16,128,640]{3,2,1,0:T(8,128)S(1)}) fusion(bf16[2,640,16,128]{3,2,1,0:T(8,128)(2,1)S(1)} %bitcast.51, f32[2,128,16,128]{1,3,2,0:T(8,128)} %get-tuple-element.180, f32[16,128]{1,0:T(8,128)S(1)} %bitcast.63, f32[2,128,16]{1,2,0:T(8,128)S(1)} %add_rsqrt_fusion), kind=kOutput, calls=%fused_computation.6 | convolution fusion | flops 677900288 | bytes 17866752 | tf_op jit(solution)/shard_map/sqhd,skhd->shqk/dot_general | solution.py:65
  454.4 2.5 fusion.3
  456.9 1.4 copy-done
  458.3 7.6 %fusion.15 = bf16[2,128,16,128]{1,3,2,0:T(8,128)(2,1)} fusion(f32[2,16,128,640]{3,2,1,0:T(8,128)} %copy-done, f32[2,16,128]{2,1,0:T(8,128)S(1)} %get-tuple-element.181, bf16[2,640,16,128]{3,2,1,0:T(8,128)(2,1)S(1)} %bitcast.58, f32[2,128,16]{1,2,0:T(8,128)S(1)} %bitcast.64), kind=kOutput, calls=%fused_computation.23 | convolution fusion | flops 680001536 | bytes 16809984 | tf_op jit(solution)/shard_map/shqk,skhd->sqhd/dot_general | solution.py:72
  466.0 2.3 copy.23
  (43 shorter events, 13.7 us)
Async XLA Ops:
  6.5 35.2 %all-gather.5.cloned.1.call-start = ((), (), s32[]{:S(2)}) async-start(), calls=%async_computation | async-start | bytes 25165824 | tf_op jit(solution)/shard_map/all_gather | solution.py:27
  7.3 67.3 %all-gather.7.cloned.1.call-start = ((), (), s32[]{:S(2)}) async-start(), calls=%async_computation.1 | async-start | bytes 25165824 | tf_op jit(solution)/shard_map/all_gather | solution.py:28
  8.0 1.6 copy-start.2
  8.0 2.1 copy-start.5
  8.0 99.3 %all-gather.11.cloned.1.call-start = ((), (), s32[]{:S(2)}) async-start(), calls=%async_computation.3 | async-start | bytes 25165824 | tf_op jit(solution)/shard_map/all_gather | solution.py:26
  8.8 329.5 %all-gather.9.cloned.1.call-start = ((), (), s32[]{:S(2)}) async-start(), calls=%async_computation.2 | async-start | bytes 18874368 | tf_op jit(solution)/shard_map/all_gather | solution.py:44
  41.7 32.8 %copy-start.3 = (bf16[2,128,4096]{2,1,0:T(8,128)(2,1)S(1)}, bf16[2,128,4096]{2,1,0:T(8,128)(2,1)}, u32[]{:S(2)}) copy-start(bf16[2,128,4096]{2,1,0:T(8,128)(2,1)} %fusion.14) | copy-start | bytes 6291460
  85.5 12.1 %copy-start.6 = (f32[2048]{0:T(1024)S(1)}, f32[2048]{0:T(1024)}, u32[]{:S(2)}) copy-start(f32[2048]{0:T(1024)} %param.16) | copy-start | bytes 24580
  360.1 5.3 %copy-start.7 = (s32[1,5]{1,0:T(1,128)S(1)}, s32[1,5]{1,0:T(1,128)}, u32[]{:S(2)}) copy-start(s32[1,5]{1,0:T(1,128)} %param.17) | copy-start | bytes 64
  442.7 4.4 copy-start.1
  447.1 1.8 copy-start.4
  454.4 4.0 copy-start
Sparse Core Ops, SparseCore 0:
  8.9 32.7 all-gather.4
  43.3 31.2 all-gather.6
  76.1 31.2 all-gather.10
  109.3 228.9 all-gather.8
where the time goes:
time: 477 us; the launch traced here: 475 us
  waiting for transfers between devices  251 us (53%)
  local copies, waits for them, and re-layouts  93 us (19%)
  other arithmetic  58.7 us (12%)
  matrix products  43.4 us (9%)
  loops' own time  15.3 us (3%)
  between operations  13.3 us (3%)
    all_gather x1, waiting for transfers between devices, shards(): piece = lax.all_gather(key_value, 'ctx', axis=2, tiled=True)  201 us
    dot_general x2, local copies, waits for them, and re-layouts, shards(): jnp.dot(flat_rows, piece, preferred_element_type=jnp.float32)  43.2 us
    dynamic_update_slice x8, other arithmetic, put_one(): lax.dynamic_update_slice_in_dim(current_store, jnp.where(present, arrivin...  41.3 us
    dot_general x3, matrix products, shards(): jnp.dot(flat_rows, piece, preferred_element_type=jnp.float32)  30.4 us
    all_gather x1, waiting for transfers between devices, shards(): lax.all_gather(w_key, 'dp', axis=0, tiled=True)  29.6 us
    all_gather x1, local copies, waits for them, and re-layouts, shards(): piece = lax.all_gather(key_value, 'ctx', axis=2, tiled=True)  21.9 us
    another operation x1, loops' own time, shards(): slot_store = lax.fori_loop(0, block_count, put_one, slot_store)  15.3 us
    all_gather x1, waiting for transfers between devices, shards(): lax.all_gather(w_value, 'dp', axis=0, tiled=True)  10.7 us
  transfers between devices with their start and end apart: 4, of which 4 were waited for; matrix products, arithmetic and copies ran while one was open for 17% of the time, Pallas kernels for 0%

commit v1 on v0

v1 whole, which is shorter than its diff:
```python
import functools

import jax
import jax.numpy as jnp
from jax import lax
from jax.experimental import pallas as pl
from jax.experimental.pallas import tpu as pltpu
from jax.sharding import PartitionSpec as P

HEAD_DIM = 128
EPS = 1e-06
LAG = 2
MESH = pl.DeviceIdType.MESH


def fused(
    n,
    tok_hbm, gain_ref, wq_hbm, wk_hbm, wv_hbm, qg_ref, kg_ref, kb_hbm,
    out_ref,
    tok, lhs, xsend, wbuf, pmine, psend, precv, send, recv_a, recv_b, obuf, kb_all, kb_smem,
    tok_sem, w_sem, x_ssem, x_rsem, p_ssem, p_rsem, a_ssem, a_rsem, o_ssem, o_rsem,
    kb_ssem, kb_rsem, kb_lsem,
):
    c = lax.axis_index("ctx")
    d = lax.axis_index("dp")
    seqs, rows, width = tok.shape
    half = width // 2
    cw = wbuf.shape[2] // 3
    heads = cw // HEAD_DIM
    recvs = (recv_a, recv_b)
    steps = seqs * n

    def peer(t):
        odd = t % 2
        off = n // 2 + (1 - odd) * (t // 2) - odd * ((t + 1) // 2)
        return (c + off) % n

    def tok_copy(s):
        return pltpu.make_async_copy(tok_hbm.at[s], tok.at[s], tok_sem.at[s])

    def w_copy(j, i):
        w = (wq_hbm, wk_hbm, wv_hbm)[i]
        return pltpu.make_async_copy(
            w.at[:, pl.ds(pl.multiple_of(j * cw, cw), cw)],
            wbuf.at[j, :, pl.ds(i * cw, cw)],
            w_sem.at[j, i],
        )

    def x_copy(s):
        return pltpu.make_async_remote_copy(
            src_ref=xsend.at[s], dst_ref=lhs.at[s, pl.ds(rows, rows)],
            send_sem=x_ssem.at[s], recv_sem=x_rsem.at[s],
            device_id={"dp": 1 - d}, device_id_type=MESH)

    def p_copy(u):
        return pltpu.make_async_remote_copy(
            src_ref=psend.at[u], dst_ref=precv.at[u],
            send_sem=p_ssem.at[u], recv_sem=p_rsem.at[u],
            device_id={"dp": 1 - d}, device_id_type=MESH)

    def a_copy(s, j, src):
        return pltpu.make_async_remote_copy(
            src_ref=send.at[s, j], dst_ref=recvs[s].at[src],
            send_sem=a_ssem.at[s, j], recv_sem=a_rsem.at[s, src],
            device_id={"ctx": j}, device_id_type=MESH)

    def o_copy(s, j, src):
        return pltpu.make_async_remote_copy(
            src_ref=obuf.at[s, j],
            dst_ref=out_ref.at[s, :, pl.ds(pl.multiple_of(src * cw, cw), cw)],
            send_sem=o_ssem.at[s, j], recv_sem=o_rsem.at[s, src],
            device_id={"ctx": j}, device_id_type=MESH)

    def kb_copy(j, src):
        return pltpu.make_async_remote_copy(
            src_ref=kb_hbm, dst_ref=kb_all.at[src],
            send_sem=kb_ssem.at[j], recv_sem=kb_rsem.at[src],
            device_id={"ctx": j}, device_id_type=MESH)

    for s in range(seqs):
        tok_copy(s).start()

    def start_weights(t, _):
        for i in range(3):
            w_copy(peer(t), i).start()
        return 0

    lax.fori_loop(0, n, start_weights, 0)

    barrier = pltpu.get_barrier_semaphore()
    pl.semaphore_signal(barrier, inc=1, device_id={"dp": 1 - d}, device_id_type=MESH)

    def greet(t, _):
        pl.semaphore_signal(barrier, inc=1, device_id={"ctx": peer(t)}, device_id_type=MESH)
        return 0

    lax.fori_loop(0, n - 1, greet, 0)

    mine = pl.ds(pl.multiple_of(d * half, half), half)
    other = pl.ds(pl.multiple_of((1 - d) * half, half), half)
    tile = 16
    for s in range(seqs):
        tok_copy(s).wait()

        def norm_rows(r, _):
            at = pl.ds(pl.multiple_of(r * tile, tile), tile)
            a = tok[s, at, mine].astype(jnp.float32)
            b = tok[s, at, other].astype(jnp.float32)
            total = jnp.sum(a * a, axis=-1, keepdims=True) + jnp.sum(b * b, axis=-1, keepdims=True)
            scale = lax.rsqrt(total * (1.0 / width) + EPS)
            lhs[s, at, :] = (a * scale * gain_ref[:, mine]).astype(jnp.bfloat16)
            xsend[s, at, :] = (b * scale * gain_ref[:, other]).astype(jnp.bfloat16)
            return 0

        lax.fori_loop(0, rows // tile, norm_rows, 0)
        if s == 0:
            pl.semaphore_wait(barrier, n)
        x_copy(s).start()

    def send_kb(t, _):
        kb_copy(peer(t), c).start()
        return 0

    lax.fori_loop(0, n - 1, send_kb, 0)
    pltpu.make_async_copy(kb_hbm, kb_all.at[c], kb_rsem.at[c]).start()

    def project(s, _):
        def step(t, _):
            @pl.when(t < n)
            def _():
                j = peer(t)
                u = s * n + t

                @pl.when(t == 0)
                def _():
                    x_copy(s).wait_recv()

                @pl.when(s == 0)
                def _():
                    for i in range(3):
                        w_copy(j, i).wait()

                acc = jnp.dot(lhs[s], wbuf[j], preferred_element_type=jnp.float32)
                psend[u] = acc[rows:]
                p_copy(u).start()
                pmine[t % (LAG + 1)] = acc[:rows]

            @pl.when(t >= LAG)
            def _():
                v = t - LAG
                j = peer(v)
                u = s * n + v
                p_copy(u).wait_recv()
                slot = v % (LAG + 1)
                for i, g_ref in enumerate((qg_ref, kg_ref)):
                    for h in range(heads):
                        at = pl.ds(i * cw + h * HEAD_DIM, HEAD_DIM)
                        raw = pmine[slot, :, at] + precv[u, :, at]
                        ms = jnp.mean(raw * raw, axis=-1, keepdims=True)
                        gains = g_ref[:, pl.ds(pl.multiple_of(j * cw + h * HEAD_DIM, HEAD_DIM), HEAD_DIM)]
                        send[s, j, :, at] = (raw * lax.rsqrt(ms + EPS) * gains).astype(jnp.bfloat16)
                at = pl.ds(2 * cw, cw)
                send[s, j, :, at] = (pmine[slot, :, at] + precv[u, :, at]).astype(jnp.bfloat16)

                @pl.when(v < n - 1)
                def _():
                    a_copy(s, j, c).start()

                @pl.when(v == n - 1)
                def _():
                    pltpu.make_async_copy(send.at[s, c], recvs[s].at[c], a_rsem.at[s, c]).start()

            return 0

        lax.fori_loop(0, n + LAG, step, 0)

    for s in range(seqs):
        project(s, 0)

    def wait_kb(j, _):
        kb_copy(j, j).wait_recv()
        return 0

    lax.fori_loop(0, n, wait_kb, 0)
    lists = pltpu.make_async_copy(kb_all, kb_smem, kb_lsem)
    lists.start()
    lists.wait()

    scale = 1.0 / float(HEAD_DIM) ** 0.5
    slots = 5
    for s in range(seqs):
        recv = recvs[s]

        def wait_block(j, _):
            a_copy(s, j, j).wait_recv()
            return 0

        lax.fori_loop(0, n, wait_block, 0)

        def attend(t, _):
            b = peer(t)
            listed = [kb_smem[b, 0, i] for i in range(slots)]
            for h in range(heads):
                lo = h * HEAD_DIM
                q = recv[b, :, pl.ds(lo, HEAD_DIM)]
                scores = []
                for kb in listed:
                    k = recv[kb, :, pl.ds(cw + lo, HEAD_DIM)]
                    scores.append(
                        lax.dot_general(q, k, (((1,), (1,)), ((), ())), preferred_element_type=jnp.float32) * scale
                    )
                top = functools.reduce(jnp.maximum, scores)
                row_max = jnp.max(top, axis=-1, keepdims=True)
                expo = [jnp.exp(x - row_max) for x in scores]
                total = jnp.sum(functools.reduce(jnp.add, expo), axis=-1, keepdims=True)
                mixed = None
                for e, kb in zip(expo, listed):
                    v = recv[kb, :, pl.ds(2 * cw + lo, HEAD_DIM)]
                    part = jnp.dot(e.astype(jnp.bfloat16), v, preferred_element_type=jnp.float32)
                    mixed = part if mixed is None else mixed + part
                obuf[s, b, :, pl.ds(lo, HEAD_DIM)] = (mixed / total).astype(jnp.bfloat16)

            @pl.when(t < n - 1)
            def _():
                o_copy(s, b, c).start()

            @pl.when(t == n - 1)
            def _():
                pltpu.make_async_copy(
                    obuf.at[s, c],
                    out_ref.at[s, :, pl.ds(pl.multiple_of(c * cw, cw), cw)],
                    o_rsem.at[s, c],
                ).start()

            return 0

        lax.fori_loop(0, n, attend, 0)

    def drain_p(u, _):
        p_copy(u).wait_send()
        return 0

    lax.fori_loop(0, steps, drain_p, 0)

    def drain_kb(t, _):
        kb_copy(peer(t), c).wait_send()
        return 0

    lax.fori_loop(0, n - 1, drain_kb, 0)
    for s in range(seqs):
        x_copy(s).wait_send()

        def drain(t, _):
            j = peer(t)
            a_copy(s, j, c).wait_send()
            o_copy(s, j, c).wait_send()
            return 0

        lax.fori_loop(0, n - 1, drain, 0)

        def arrive(j, _):
            o_copy(s, j, j).wait_recv()
            return 0

        lax.fori_loop(0, n, arrive, 0)


def shards(n, tokens, norm_gain, w_query, w_key, w_value, query_gain, key_gain, key_blocks):
    seqs, rows, width = tokens.shape
    half, hh = w_query.shape
    cw = hh // n
    bf, f32 = jnp.bfloat16, jnp.float32
    lists = jnp.pad(key_blocks, ((0, 7), (0, 128 - key_blocks.shape[1])))
    hbm = pl.BlockSpec(memory_space=pl.ANY)
    vmem = pl.BlockSpec(memory_space=pltpu.VMEM)
    dma = pltpu.SemaphoreType.DMA
    return pl.pallas_call(
        functools.partial(fused, n),
        out_shape=jax.ShapeDtypeStruct((seqs, rows, hh), bf),
        in_specs=[hbm, vmem, hbm, hbm, hbm, vmem, vmem, hbm],
        out_specs=hbm,
        scratch_shapes=[
            pltpu.VMEM((seqs, rows, width), bf),
            pltpu.VMEM((seqs, 2 * rows, half), bf),
            pltpu.VMEM((seqs, rows, half), bf),
            pltpu.VMEM((n, half, 3 * cw), bf),
            pltpu.VMEM((LAG + 1, rows, 3 * cw), f32),
            pltpu.VMEM((seqs * n, rows, 3 * cw), f32),
            pltpu.VMEM((seqs * n, rows, 3 * cw), f32),
            pltpu.VMEM((seqs, n, rows, 3 * cw), bf),
            pltpu.VMEM((n, rows, 3 * cw), bf),
            pltpu.VMEM((n, rows, 3 * cw), bf),
            pltpu.VMEM((seqs, n, rows, cw), bf),
            pltpu.VMEM((n, 8, 128), jnp.int32),
            pltpu.SMEM((n, 8, 128), jnp.int32),
            dma((seqs,)),
            dma((n, 3)),
            dma((seqs,)),
            dma((seqs,)),
            dma((seqs * n,)),
            dma((seqs * n,)),
            dma((seqs, n)),
            dma((seqs, n)),
            dma((seqs, n)),
            dma((seqs, n)),
            dma((n,)),
            dma((n,)),
            dma(()),
        ],
        compiler_params=pltpu.CompilerParams(
            collective_id=0, has_side_effects=True, vmem_limit_bytes=60 * 1024 * 1024
        ),
    )(
        tokens, norm_gain.reshape(1, width), w_query, w_key, w_value,
        query_gain.reshape(1, hh), key_gain.reshape(1, hh), lists,
    )


def solution(mesh):
    in_specs = (
        P(("groups", "dp"), "ctx", None),
        P(),
        P("dp", None),
        P("dp", None),
        P("dp", None),
        P(),
        P(),
        P(("groups", "ctx"), None),
    )
    out_specs = P(("groups", "dp"), "ctx", None)
    return jax.shard_map(
        functools.partial(shards, mesh.shape["ctx"]),
        mesh=mesh, in_specs=in_specs, out_specs=out_specs, check_vma=False,
    )
```

time: 477 us -> 108 us (0.23)
  waiting for transfers between devices: 251 us -> 0 us
  Pallas kernels: 0 us -> 104 us
  local copies, waits for them, and re-layouts: 93 us -> 3.56 us
  other arithmetic: 58.7 us -> 0 us
  matrix products: 43.4 us -> 0 us
  loops' own time: 15.3 us -> 0 us
  between operations: 13.3 us -> 0.01 us
    all_gather x4 -> x0, waiting for transfers between devices: 249 us -> none  [the longest x1 201 us: shards(): piece = lax.all_gather(key_value, 'ctx', axis=2, tiled=True)]
    pallas_call x0 -> x1, Pallas kernels: none -> 104 us  [shards(): pl.pallas_call(functools.partial(fused, n), out_shape=jax.ShapeDtypeStruc...]
    dot_general x5 -> x0, matrix products: 43.4 us -> none  [the longest x3 30.4 us: shards(): jnp.dot(flat_rows, piece, preferred_element_type=jnp.float32)]
    dot_general x2 -> x0, local copies, waits for them, and re-layouts: 43.2 us -> none  [shards(): jnp.dot(flat_rows, piece, preferred_element_type=jnp.float32)]
    dynamic_update_slice x8 -> x0, other arithmetic: 41.3 us -> none  [put_one(): lax.dynamic_update_slice_in_dim(current_store, jnp.where(present, arrivin...]
    all_gather x1 -> x0, local copies, waits for them, and re-layouts: 21.9 us -> none  [shards(): piece = lax.all_gather(key_value, 'ctx', axis=2, tiled=True)]
    another operation x1 -> x0, loops' own time: 15.3 us -> none  [shards(): slot_store = lax.fori_loop(0, block_count, put_one, slot_store)]
    slice x1 -> x0, local copies, waits for them, and re-layouts: 10.2 us -> none  [shards(): slot_store[1]]
  transfers between devices with their start and end apart: 4 -> 0, of which waited for: 4 -> 0; matrix products, arithmetic and copies ran while one was open for 17% -> 0% of each run, Pallas kernels for 0% -> 0%
where the time goes in v1:
time: 108 us; the launch traced here: 107 us
  Pallas kernels  104 us (96%)
  local copies, waits for them, and re-layouts  3.56 us (3%)
    pallas_call x1, Pallas kernels, shards(): pl.pallas_call(functools.partial(fused, n), out_shape=jax.ShapeDtypeStruc...  104 us
    unnamed x1, local copies, waits for them, and re-layouts  2.3 us

profile of v1, /device:TPU:0, one launch (start us, length us, event | category | flops | bytes accessed | tf_op | source)
XLA Modules:
  0.0 107.4 jit_solution(17516463700661522326)
XLA Ops:
  0.0 1.3 %pad.4.kb_hbm = s32[8,128]{1,0:T(8,128)} pad(s32[1,5]{1,0:T(1,128)} %param.15, s32[]{:T(128)} %constant.0.clone.1), padding=0_7x0_123 | pad | bytes 4120 | tf_op jit(solution)/shard_map/jit(_pad)/pad | solution.py:273
  1.3 103.8 %shard_map.82 = bf16[2,128,2048]{2,1,0:T(8,128)(2,1)} custom-call(bf16[2,128,4096]{2,1,0:T(8,128)(2,1)} %tok_hbm.1, f32[1,4096]{1,0:T(1,128)} %bitcast.3, bf16[2048,2048]{1,0:T(8,128)(2,1)} %wq_hbm.1, bf16[2048,2048]{1,0:T(8,128)(2,1)} %wk_hbm.1, bf16[2048,2048]{1,0:T(8,128)(2,1)} %wv_hbm.1, f32[1,2048]{1,0:T(1,128)} %bitcast.4, f32[1,2048]{1,0:T(1,128)} %bitcast.5, ...), custom_call_target="tpu_custom_call" | custom-call | tf_op jit(solution)/shard_map/pallas_call | solution.py:277
  105.1 2.3 %copy.10 = bf16[2,128,2048]{2,1,0:T(8,128)(2,1)} copy(bf16[2,128,2048]{2,1,0:T(8,128)(2,1)} %shard_map.82) | data formatting | bytes 2097152

commit v2 on v1

--- a/solution.py
+++ b/solution.py
@@ -17,9 +17,9 @@
     n,
     tok_hbm, gain_ref, wq_hbm, wk_hbm, wv_hbm, qg_ref, kg_ref, kb_hbm,
     out_ref,
-    tok, lhs, xsend, wbuf, pmine, psend, precv, send, recv_a, recv_b, obuf, kb_all, kb_smem,
+    tok, lhs, xkeep, xsend, wbuf, pmine, psend, precv, send, recv_a, recv_b, obuf, kb_all, kb_smem,
     tok_sem, w_sem, x_ssem, x_rsem, p_ssem, p_rsem, a_ssem, a_rsem, o_ssem, o_rsem,
-    kb_ssem, kb_rsem, kb_lsem,
+    kb_ssem, kb_rsem, kb_lsem, xf_ssem, xf_rsem,
 ):
     c = lax.axis_index("ctx")
     d = lax.axis_index("dp")
@@ -29,11 +29,24 @@
     heads = cw // HEAD_DIM
     recvs = (recv_a, recv_b)
     steps = seqs * n
+    m = n // 2
+    z = c // m
+    across = (c + m) % n
+    near = d == z
+    far = d != z
+    share = (c - z * m) * 2 + d
+    block_a = (c + (d + z) % 2 * m) % n
 
     def peer(t):
         odd = t % 2
         off = n // 2 + (1 - odd) * (t // 2) - odd * ((t + 1) // 2)
         return (c + off) % n
+
+    def peer_a(t):
+        return ((c - z * m) * 2 + 2 + t) % n
+
+    def chunk_at(s, t):
+        return peer_a(t) if s == 0 else peer(t)
 
     def tok_copy(s):
         return pltpu.make_async_copy(tok_hbm.at[s], tok.at[s], tok_sem.at[s])
@@ -58,7 +71,24 @@
             send_sem=p_ssem.at[u], recv_sem=p_rsem.at[u],
             device_id={"dp": 1 - d}, device_id_type=MESH)
 
+    def xf_copy(src_ref, at, send_sem, recv_sem, core):
+        return pltpu.make_async_remote_copy(
+            src_ref=src_ref, dst_ref=lhs.at[0, pl.ds(at, rows)],
+            send_sem=send_sem, recv_sem=recv_sem,
+            device_id={"ctx": across, "dp": core}, device_id_type=MESH)
+
+    def xf_keep():
+        return xf_copy(xkeep, rows, xf_ssem, x_rsem.at[0], d)
+
+    def xf_send():
+        return xf_copy(xsend.at[0], 0, x_ssem.at[0], xf_rsem, 1 - d)
+
     def a_copy(s, j, src):
+        if s == 0:
+            return pltpu.make_async_remote_copy(
+                src_ref=send.at[0, j], dst_ref=recv_a.at[src],
+                send_sem=a_ssem.at[0, j], recv_sem=a_rsem.at[0, src],
+                device_id={"ctx": z * m + j // 2, "dp": j % 2}, device_id_type=MESH)
         return pltpu.make_async_remote_copy(
             src_ref=send.at[s, j], dst_ref=recvs[s].at[src],
             send_sem=a_ssem.at[s, j], recv_sem=a_rsem.at[s, src],
@@ -69,7 +99,7 @@
             src_ref=obuf.at[s, j],
             dst_ref=out_ref.at[s, :, pl.ds(pl.multiple_of(src * cw, cw), cw)],
             send_sem=o_ssem.at[s, j], recv_sem=o_rsem.at[s, src],
-            device_id={"ctx": j}, device_id_type=MESH)
+            device_id={"ctx": j, "dp": z} if s == 0 else {"ctx": j}, device_id_type=MESH)
 
     def kb_copy(j, src):
         return pltpu.make_async_remote_copy(
@@ -88,7 +118,13 @@
     lax.fori_loop(0, n, start_weights, 0)
 
     barrier = pltpu.get_barrier_semaphore()
-    pl.semaphore_signal(barrier, inc=1, device_id={"dp": 1 - d}, device_id_type=MESH)
+
+    def greet_other(t, _):
+        pl.semaphore_signal(
+            barrier, inc=1, device_id={"ctx": peer(t), "dp": 1 - d}, device_id_type=MESH)
+        return 0
+
+    lax.fori_loop(0, n, greet_other, 0)
 
     def greet(t, _):
         pl.semaphore_signal(barrier, inc=1, device_id={"ctx": peer(t)}, device_id_type=MESH)
@@ -108,14 +144,26 @@
             b = tok[s, at, other].astype(jnp.float32)
             total = jnp.sum(a * a, axis=-1, keepdims=True) + jnp.sum(b * b, axis=-1, keepdims=True)
             scale = lax.rsqrt(total * (1.0 / width) + EPS)
-            lhs[s, at, :] = (a * scale * gain_ref[:, mine]).astype(jnp.bfloat16)
+            held = xkeep if s == 0 else lhs.at[s]
+            held[at, :] = (a * scale * gain_ref[:, mine]).astype(jnp.bfloat16)
             xsend[s, at, :] = (b * scale * gain_ref[:, other]).astype(jnp.bfloat16)
             return 0
 
         lax.fori_loop(0, rows // tile, norm_rows, 0)
         if s == 0:
-            pl.semaphore_wait(barrier, n)
-        x_copy(s).start()
+            pl.semaphore_wait(barrier, 2 * n - 1)
+
+            @pl.when(far)
+            def _():
+                xf_send().start()
+                xf_keep().start()
+
+            @pl.when(near)
+            def _():
+                x_copy(0).start()
+                pltpu.make_async_copy(xkeep, lhs.at[0, pl.ds(0, rows)], xf_rsem).start()
+        else:
+            x_copy(s).start()
 
     def send_kb(t, _):
         kb_copy(peer(t), c).start()
@@ -128,15 +176,16 @@
         def step(t, _):
             @pl.when(t < n)
             def _():
-                j = peer(t)
+                j = chunk_at(s, t)
                 u = s * n + t
 
                 @pl.when(t == 0)
                 def _():
                     x_copy(s).wait_recv()
-
-                @pl.when(s == 0)
-                def _():
+                    if s == 0:
+                        xf_send().wait_recv()
+
+                if s == seqs - 1:
                     for i in range(3):
                         w_copy(j, i).wait()
 
@@ -148,7 +197,7 @@
             @pl.when(t >= LAG)
             def _():
                 v = t - LAG
-                j = peer(v)
+                j = chunk_at(s, v)
                 u = s * n + v
                 p_copy(u).wait_recv()
                 slot = v % (LAG + 1)
@@ -162,19 +211,22 @@
                 at = pl.ds(2 * cw, cw)
                 send[s, j, :, at] = (pmine[slot, :, at] + precv[u, :, at]).astype(jnp.bfloat16)
 
-                @pl.when(v < n - 1)
+                leaves = j != share if s == 0 else v < n - 1
+
+                @pl.when(leaves)
                 def _():
-                    a_copy(s, j, c).start()
-
-                @pl.when(v == n - 1)
+                    a_copy(s, j, block_a if s == 0 else c).start()
+
+                @pl.when(jnp.logical_not(leaves))
                 def _():
-                    pltpu.make_async_copy(send.at[s, c], recvs[s].at[c], a_rsem.at[s, c]).start()
+                    own = block_a if s == 0 else c
+                    pltpu.make_async_copy(send.at[s, j], recvs[s].at[own], a_rsem.at[s, own]).start()
 
             return 0
 
         lax.fori_loop(0, n + LAG, step, 0)
 
-    for s in range(seqs):
+    for s in reversed(range(seqs)):
         project(s, 0)
 
     def wait_kb(j, _):
@@ -188,8 +240,9 @@
 
     scale = 1.0 / float(HEAD_DIM) ** 0.5
     slots = 5
-    for s in range(seqs):
+    for s in reversed(range(seqs)):
         recv = recvs[s]
+        part = share if s == 0 else c
 
         def wait_block(j, _):
             a_copy(s, j, j).wait_recv()
@@ -216,20 +269,22 @@
                 mixed = None
                 for e, kb in zip(expo, listed):
                     v = recv[kb, :, pl.ds(2 * cw + lo, HEAD_DIM)]
-                    part = jnp.dot(e.astype(jnp.bfloat16), v, preferred_element_type=jnp.float32)
-                    mixed = part if mixed is None else mixed + part
+                    piece = jnp.dot(e.astype(jnp.bfloat16), v, preferred_element_type=jnp.float32)
+                    mixed = piece if mixed is None else mixed + piece
                 obuf[s, b, :, pl.ds(lo, HEAD_DIM)] = (mixed / total).astype(jnp.bfloat16)
 
-            @pl.when(t < n - 1)
-            def _():
-                o_copy(s, b, c).start()
-
-            @pl.when(t == n - 1)
+            remote = (t < n - 1) | far if s == 0 else t < n - 1
+
+            @pl.when(remote)
+            def _():
+                o_copy(s, b, part).start()
+
+            @pl.when(jnp.logical_not(remote))
             def _():
                 pltpu.make_async_copy(
                     obuf.at[s, c],
-                    out_ref.at[s, :, pl.ds(pl.multiple_of(c * cw, cw), cw)],
-                    o_rsem.at[s, c],
+                    out_ref.at[s, :, pl.ds(pl.multiple_of(part * cw, cw), cw)],
+                    o_rsem.at[s, part],
                 ).start()
 
             return 0
@@ -247,13 +302,18 @@
         return 0
 
     lax.fori_loop(0, n - 1, drain_kb, 0)
+
+    @pl.when(far)
+    def _():
+        xf_keep().wait_send()
+        o_copy(0, c, share).wait_send()
+
     for s in range(seqs):
         x_copy(s).wait_send()
 
         def drain(t, _):
-            j = peer(t)
-            a_copy(s, j, c).wait_send()
-            o_copy(s, j, c).wait_send()
+            a_copy(s, (share + 1 + t) % n if s == 0 else peer(t), c).wait_send()
+            o_copy(s, peer(t), c).wait_send()
             return 0
 
         lax.fori_loop(0, n - 1, drain, 0)
@@ -282,6 +342,7 @@
         scratch_shapes=[
             pltpu.VMEM((seqs, rows, width), bf),
             pltpu.VMEM((seqs, 2 * rows, half), bf),
+            pltpu.VMEM((rows, half), bf),
             pltpu.VMEM((seqs, rows, half), bf),
             pltpu.VMEM((n, half, 3 * cw), bf),
             pltpu.VMEM((LAG + 1, rows, 3 * cw), f32),
@@ -306,6 +367,8 @@
             dma((n,)),
             dma((n,)),
             dma(()),
+            dma(()),
+            dma(()),
         ],
         compiler_params=pltpu.CompilerParams(
             collective_id=0, has_side_effects=True, vmem_limit_bytes=60 * 1024 * 1024

time: 108 us -> 105 us (0.972)
  Pallas kernels: 104 us -> 100 us
    pallas_call x1, Pallas kernels: 104 us -> 100 us  [shards(): pl.pallas_call(functools.partial(fused, n), out_shape=jax.ShapeDtypeStruc...]
where the time goes in v2:
time: 105 us; the launch traced here: 104 us
  Pallas kernels  100 us (95%)
  local copies, waits for them, and re-layouts  3.56 us (3%)
    pallas_call x1, Pallas kernels, shards(): pl.pallas_call(functools.partial(fused, n), out_shape=jax.ShapeDtypeStruc...  100 us
    unnamed x1, local copies, waits for them, and re-layouts  2.3 us

profile of v2, /device:TPU:0, one launch (start us, length us, event | category | flops | bytes accessed | tf_op | source)
XLA Modules:
  0.0 103.5 jit_solution(5843806462323380406)
XLA Ops:
  0.0 1.3 %pad.4.kb_hbm = s32[8,128]{1,0:T(8,128)} pad(s32[1,5]{1,0:T(1,128)} %param.15, s32[]{:T(128)} %constant.0.clone.1), padding=0_7x0_123 | pad | bytes 4120 | tf_op jit(solution)/shard_map/jit(_pad)/pad | solution.py:333
  1.3 100.0 %shard_map.82 = bf16[2,128,2048]{2,1,0:T(8,128)(2,1)} custom-call(bf16[2,128,4096]{2,1,0:T(8,128)(2,1)} %tok_hbm.1, f32[1,4096]{1,0:T(1,128)} %bitcast.3, bf16[2048,2048]{1,0:T(8,128)(2,1)} %wq_hbm.1, bf16[2048,2048]{1,0:T(8,128)(2,1)} %wk_hbm.1, bf16[2048,2048]{1,0:T(8,128)(2,1)} %wv_hbm.1, f32[1,2048]{1,0:T(1,128)} %bitcast.4, f32[1,2048]{1,0:T(1,128)} %bitcast.5, ...), custom_call_target="tpu_custom_call" | custom-call | tf_op jit(solution)/shard_map/pallas_call | solution.py:337
  101.2 2.3 %copy.10 = bf16[2,128,2048]{2,1,0:T(8,128)(2,1)} copy(bf16[2,128,2048]{2,1,0:T(8,128)(2,1)} %shard_map.82) | data formatting | bytes 2097152

commit v3 on v2

--- a/solution.py
+++ b/solution.py
@@ -172,6 +172,15 @@
     lax.fori_loop(0, n - 1, send_kb, 0)
     pltpu.make_async_copy(kb_hbm, kb_all.at[c], kb_rsem.at[c]).start()
 
+    def send_across(t, _):
+        j = peer(t)
+
+        @pl.when(j // m != z)
+        def _():
+            a_copy(seqs - 1, j, c).start()
+
+        return 0
+
     def project(s, _):
         def step(t, _):
             @pl.when(t < n)
@@ -184,6 +193,7 @@
                     x_copy(s).wait_recv()
                     if s == 0:
                         xf_send().wait_recv()
+                        lax.fori_loop(0, n - 1, send_across, 0)
 
                 if s == seqs - 1:
                     for i in range(3):
@@ -212,8 +222,9 @@
                 send[s, j, :, at] = (pmine[slot, :, at] + precv[u, :, at]).astype(jnp.bfloat16)
 
                 leaves = j != share if s == 0 else v < n - 1
-
-                @pl.when(leaves)
+                early = leaves if s == 0 else leaves & (j // m == z)
+
+                @pl.when(early)
                 def _():
                     a_copy(s, j, block_a if s == 0 else c).start()
 
@@ -330,7 +341,6 @@
     half, hh = w_query.shape
     cw = hh // n
     bf, f32 = jnp.bfloat16, jnp.float32
-    lists = jnp.pad(key_blocks, ((0, 7), (0, 128 - key_blocks.shape[1])))
     hbm = pl.BlockSpec(memory_space=pl.ANY)
     vmem = pl.BlockSpec(memory_space=pltpu.VMEM)
     dma = pltpu.SemaphoreType.DMA
@@ -352,8 +362,8 @@
             pltpu.VMEM((n, rows, 3 * cw), bf),
             pltpu.VMEM((n, rows, 3 * cw), bf),
             pltpu.VMEM((seqs, n, rows, cw), bf),
-            pltpu.VMEM((n, 8, 128), jnp.int32),
-            pltpu.SMEM((n, 8, 128), jnp.int32),
+            pltpu.VMEM((n,) + key_blocks.shape, jnp.int32),
+            pltpu.SMEM((n,) + key_blocks.shape, jnp.int32),
             dma((seqs,)),
             dma((n, 3)),
             dma((seqs,)),
@@ -375,7 +385,7 @@
         ),
     )(
         tokens, norm_gain.reshape(1, width), w_query, w_key, w_value,
-        query_gain.reshape(1, hh), key_gain.reshape(1, hh), lists,
+        query_gain.reshape(1, hh), key_gain.reshape(1, hh), key_blocks,
     )
 
 

time: 105 us -> 100 us (0.952)
  the two profiles are of different devices: /device:TPU:0 before, /device:TPU:18 now
where the time goes in v3:
time: 100 us
  Pallas kernels  97.7 us (98%)
  local copies, waits for them, and re-layouts  2.3 us (2%)
    pallas_call x1, Pallas kernels, shards(): pl.pallas_call(functools.partial(fused, n), out_shape=jax.ShapeDtypeStruc...  97.7 us
    unnamed x1, local copies, waits for them, and re-layouts  2.3 us

profile of v3, /device:TPU:18, one launch (start us, length us, event | category | flops | bytes accessed | tf_op | source)
XLA Modules:
  0.0 100.1 jit_solution(15300295813125551320)
XLA Ops:
  0.0 97.7 %shard_map.82 = bf16[2,128,2048]{2,1,0:T(8,128)(2,1)} custom-call(bf16[2,128,4096]{2,1,0:T(8,128)(2,1)} %tok_hbm.1, f32[1,4096]{1,0:T(1,128)} %bitcast.3, bf16[2048,2048]{1,0:T(8,128)(2,1)} %wq_hbm.1, bf16[2048,2048]{1,0:T(8,128)(2,1)} %wk_hbm.1, bf16[2048,2048]{1,0:T(8,128)(2,1)} %wv_hbm.1, f32[1,2048]{1,0:T(1,128)} %bitcast.4, f32[1,2048]{1,0:T(1,128)} %bitcast.5, ...), custom_call_target="tpu_custom_call" | custom-call | tf_op jit(solution)/shard_map/pallas_call | solution.py:347
  97.7 2.3 %copy.10 = bf16[2,128,2048]{2,1,0:T(8,128)(2,1)} copy(bf16[2,128,2048]{2,1,0:T(8,128)(2,1)} %shard_map.82) | data formatting | bytes 2097152
